TPU v7x, 256 devices: a whole 4x4x8 slice. The times are simulated.
256 devices in a mesh: gz: 8 (over y, z_lo), row: 4 (over z_hi), col: 8 (over x, core).
Axes of the slice: x: 4, y: 4, z: 8 (z_hi: 4, z_lo: 2; z = z_hi * 2 + z_lo), core: 2. Of those that a mesh axis runs over, the one named last changes fastest.
Arguments:
- lower_sub: bfloat16 [8, 2048, 8192], P('gz', 'row'), may hold values from -0.0625 to 0.0625
- upper_sub: bfloat16 [8, 8192, 2048], P('gz', None, 'col'), may hold values from -6 to 6
- block_mask: int32 [8, 16, 16], P('gz', 'row', 'col'), may hold values 0 or 1
- front_base: float32 [2048, 2048], P(('row', 'gz'), 'col'), may hold values from -6 to 6
- pivot_inverse: float32 [2, 256, 256], replicated, may hold values from -0.01 to 0.01
- pivot_order: int32 [2, 256], replicated, may hold values from 0 to 255, each once within a row
Outputs:
- factored: float32 [2048, 2048], P(('row', 'gz'), 'col')
Inputs may be any that keep to these rules, and one draw needn't show every extreme that they name: Each row of pivot_order is a permutation of 0 .. 255.
All inputs are finite; a program needn't handle non-finite values. No bound on the sum of `block_mask` on one device may be relied on, other than what follows from the above.
Results may differ from a plain program's by a relative error of at most 0.0003.
Values sent between devices are 32-bit elements; how exact they have to be, the bound alone decides.
A program may use at most 64 MiB of HBM per device.

v0:
```python
import jax
import jax.numpy as jnp
from jax import lax
from jax.sharding import PartitionSpec as P


def spread_2(block, axis, holder):
    block = jnp.where(lax.axis_index(axis) == holder, block, jnp.zeros_like(block))
    return lax.psum(block, axis)


def on_device(lower_sub, upper_sub, block_mask, front_base, pivot_inverse, pivot_order):
    highest = lax.Precision.HIGHEST
    left_factor = lower_sub[0]
    right_factor = upper_sub[0]
    slab_rows = left_factor.shape[0]
    own_rows, own_cols = front_base.shape
    tiles = block_mask[0].astype(jnp.float32)
    tile_rows = slab_rows // tiles.shape[0]
    tile_cols = own_cols // tiles.shape[1]
    spread = jnp.broadcast_to(
        tiles[:, None, :, None], (tiles.shape[0], tile_rows, tiles.shape[1], tile_cols)
    ).reshape(slab_rows, own_cols)
    summed = lax.psum_scatter(
        jnp.dot(left_factor, right_factor, preferred_element_type=jnp.float32) * spread,
        "gz",
        scatter_dimension=0,
        tiled=True,
    )
    front = front_base + summed
    block_index = lax.axis_index("row") * lax.axis_size("gz") + lax.axis_index("gz")
    row_ids = block_index * own_rows + jnp.arange(own_rows, dtype=jnp.int32)
    col_ids = lax.axis_index("col") * own_cols + jnp.arange(own_cols, dtype=jnp.int32)
    panel_width = pivot_inverse.shape[1]
    for panel in range(pivot_inverse.shape[0]):
        start_row = panel * panel_width
        after_row = start_row + panel_width
        targets = start_row + jnp.arange(panel_width, dtype=jnp.int32)
        placer = (targets[:, None] == row_ids[None, :]).astype(jnp.float32)
        owned = (row_ids >= start_row) & (row_ids < after_row)
        column_rows = lax.all_gather(front, "gz", axis=0, tiled=True)
        pivot_block = spread_2(column_rows[start_row:after_row], "row", 0)
        permuted = jnp.take(pivot_block, pivot_order[panel], axis=0)
        placed = jnp.dot(placer.T, permuted, precision=highest)
        front = jnp.where(owned[:, None], placed, front)
        root_col = start_row // own_cols
        offset = start_row - root_col * own_cols
        panel_cols = front
        beneath = row_ids >= after_row
        lower = jnp.where(
            beneath[:, None], jnp.dot(panel_cols, pivot_inverse[panel], precision=highest), 0.0
        )
        lower = spread_2(lower, "col", root_col)
        is_root = lax.axis_index("col") == root_col
        front = front.at[:, offset : offset + panel_width].set(
            jnp.where(beneath[:, None] & is_root, lower, panel_cols)
        )
        update = jnp.dot(lower, permuted, precision=highest)
        front = front - jnp.where((col_ids >= after_row)[None, :], update, 0.0)
    return front


def solution(mesh):
    placed = (
        P("gz", "row", None),
        P("gz", None, "col"),
        P("gz", "row", "col"),
        P(("row", "gz"), "col"),
        P(),
        P(),
    )
    return jax.shard_map(
        on_device, mesh=mesh, in_specs=placed, out_specs=P(("row", "gz"), "col"), check_vma=False
    )
```

profile of v0, /device:TPU:8, one launch (start us, length us, event | category | flops | bytes accessed | tf_op | source)
XLA Modules:
  0.0 361.3 jit_solution(12610471177662328038)
XLA Ops:
  6.5 0.0 reduce-scatter.2.cloned.1.call-start
  6.5 0.7 convert_bitcast_fusion
  7.2 0.1 copy.7
  7.3 0.2 broadcast_in_dim.90
  7.5 0.0 copy-start.2
  7.5 0.0 copy-start.1
  7.5 0.0 copy-start
  7.6 7.8 %fusion.3 = f32[512,256]{1,0:T(8,128)} fusion(bf16[1,8192,256]{2,1,0:T(8,128)(2,1)} %param.17, bf16[1,512,8192]{2,1,0:T(8,128)(2,1)} %param.16, f32[64,8,2,128]{3,2,1,0:T(2,128)S(1)} %bitcast.28), kind=kOutput, calls=%fused_computation.5 | convolution fusion | flops 2147614720 | bytes 13631488 | tf_op jit(solution)/shard_map/dot_general | solution.py:25
  15.3 0.0 reduce-scatter.2.cloned.1.call-update
  15.3 0.0 all-reduce.5.cloned.1.call-start
  15.5 0.0 copy-done.2
  15.5 41.5 %reduce-scatter.2.cloned.1.call-done = f32[64,256]{1,0:T(8,128)} async-done(((f32[512,256]{1,0:T(8,128)}), f32[64,256]{1,0:T(8,128)}) %reduce-scatter.2.cloned.1.call-update) | async-done | bytes 65552 | tf_op jit(solution)/shard_map/reduce_scatter | solution.py:24
  57.0 0.0 copy-done.1
  57.0 0.8 add.81
  57.9 30.0 %all_gather.6 = f32[512,256]{1,0:T(8,128)S(1)} all-gather(f32[64,256]{1,0:T(8,128)S(1)} %add.81), channel_id=1, replica_groups=mesh['gz'=8,'row'=4,'col'=8] {'gz'}, dimensions={0}, use_global_device_ids=true | all-gather | bytes 589824 | tf_op jit(solution)/shard_map/all_gather | solution.py:41
  87.8 0.7 slice_select_fusion.1
  88.5 0.0 all-reduce.5.cloned.1.call-update
  88.6 0.0 all-reduce.7.cloned.1.call-start
  88.6 51.6 %all-reduce.5.cloned.1.call-done = f32[256,256]{1,0:T(8,128)} async-done(((f32[256,256]{1,0:T(8,128)}), f32[256,256]{1,0:T(8,128)}) %all-reduce.5.cloned.1.call-update) | async-done | bytes 262160 | tf_op jit(solution)/shard_map/psum | solution.py:9
  140.2 1.9 gather_fusion
  142.1 0.3 convolution_select_fusion.5
  142.5 0.0 copy-done
  142.5 0.9 fusion.11
  143.4 0.0 all-reduce.7.cloned.1.call-update
  143.4 0.0 all-reduce.9.cloned.1.call-start
  143.5 62.5 %all-reduce.7.cloned.1.call-done = f32[64,256]{1,0:T(8,128)} async-done(((f32[64,256]{1,0:T(8,128)}), f32[64,256]{1,0:T(8,128)}) %all-reduce.7.cloned.1.call-update) | async-done | bytes 65552 | tf_op jit(solution)/shard_map/psum | solution.py:9
  206.0 1.3 fusion.10
  207.2 28.0 %all_gather.7 = f32[512,256]{1,0:T(8,128)S(1)} all-gather(f32[64,256]{1,0:T(8,128)S(1)} %fusion.10), channel_id=1, replica_groups=mesh['gz'=8,'row'=4,'col'=8] {'gz'}, dimensions={0}, use_global_device_ids=true | all-gather | bytes 589824 | tf_op jit(solution)/shard_map/all_gather | solution.py:41
  235.2 0.7 slice_select_fusion
  235.9 0.0 all-reduce.9.cloned.1.call-update
  235.9 0.0 all-reduce.11.cloned.1.call-start
  236.0 51.1 %all-reduce.9.cloned.1.call-done = f32[256,256]{1,0:T(8,128)} async-done(((f32[256,256]{1,0:T(8,128)}), f32[256,256]{1,0:T(8,128)}) %all-reduce.9.cloned.1.call-update) | async-done | bytes 262160 | tf_op jit(solution)/shard_map/psum | solution.py:9
  287.1 1.9 gather_fusion.1
  289.0 0.4 convolution_select_fusion.2
  289.4 0.9 fusion.9
  290.3 0.0 all-reduce.11.cloned.1.call-update
  290.3 62.6 %all-reduce.11.cloned.1.call-done = f32[64,256]{1,0:T(8,128)} async-done(((f32[64,256]{1,0:T(8,128)}), f32[64,256]{1,0:T(8,128)}) %all-reduce.11.cloned.1.call-update) | async-done | bytes 65552 | tf_op jit(solution)/shard_map/psum | solution.py:9
  352.9 1.9 fusion.8
  (16 shorter events, 0.1 us)
Async XLA Ops:
  6.5 50.5 %reduce-scatter.2.cloned.1.call-start = ((), (), s32[]{:S(2)}) async-start(), calls=%async_computation.1 | async-start | bytes 589824 | tf_op jit(solution)/shard_map/reduce_scatter | solution.py:24
  7.5 8.0 %copy-start.2 = (s32[2,256]{1,0:T(2,128)S(1)}, s32[2,256]{1,0:T(2,128)}, u32[]{:S(2)}) copy-start(s32[2,256]{1,0:T(2,128)} %param.21) | copy-start | bytes 6148
  7.5 49.5 %copy-start.1 = (f32[64,256]{1,0:T(8,128)S(1)}, f32[64,256]{1,0:T(8,128)}, u32[]{:S(2)}) copy-start(f32[64,256]{1,0:T(8,128)} %param.19) | copy-start | bytes 196612
  7.5 134.9 %copy-start = (f32[2,256,256]{2,1,0:T(8,128)S(1)}, f32[2,256,256]{2,1,0:T(8,128)}, u32[]{:S(2)}) copy-start(f32[2,256,256]{2,1,0:T(8,128)} %param.20) | copy-start | bytes 1572868
  15.3 124.9 %all-reduce.5.cloned.1.call-start = ((), (), s32[]{:S(2)}) async-start(), calls=%async_computation.2 | async-start | bytes 524288 | tf_op jit(solution)/shard_map/psum | solution.py:9
  88.6 117.4 %all-reduce.7.cloned.1.call-start = ((), (), s32[]{:S(2)}) async-start(), calls=%async_computation.3 | async-start | bytes 131072 | tf_op jit(solution)/shard_map/psum | solution.py:9
  143.4 143.7 %all-reduce.9.cloned.1.call-start = ((), (), s32[]{:S(2)}) async-start(), calls=%async_computation.4 | async-start | bytes 524288 | tf_op jit(solution)/shard_map/psum | solution.py:9
  235.9 117.0 %all-reduce.11.cloned.1.call-start = ((), (), s32[]{:S(2)}) async-start(), calls=%async_computation.5 | async-start | bytes 131072 | tf_op jit(solution)/shard_map/psum | solution.py:9
Sparse Core Ops, SparseCore 0:
  15.5 41.5 reduce-scatter.1
  88.7 51.4 all-reduce.4
  143.5 62.4 all-reduce.6
  236.1 50.9 all-reduce.8
  290.4 62.4 all-reduce.10
where the time goes:
time: 362 us; the launch traced here: 361 us
  waiting for transfers between devices  269 us (74%)
  blocking collectives  57.9 us (16%)
  matrix products  13.4 us (4%)
  between operations  13.3 us (4%)
  local copies, waits for them, and re-layouts  4.15 us (1%)
    psum x4, waiting for transfers between devices, spread_2(): return lax.psum(block, axis)  228 us
    all_gather x2, blocking collectives, on_device(): column_rows = lax.all_gather(front, 'gz', axis=0, tiled=True)  57.9 us
    reduce_scatter x1, waiting for transfers between devices, on_device(): lax.psum_scatter(jnp.dot(left_factor, right_factor, preferred_element_typ...  41.5 us
    dot_general x1, matrix products, on_device(): jnp.dot(left_factor, right_factor, preferred_element_type=jnp.float32)  7.75 us
  transfers between devices with their start and end apart: 5, of which 5 were waited for; matrix products, arithmetic and copies ran while one was open for 0% of the time, Pallas kernels for 0%

commit v1 on v0

--- a/solution.py
+++ b/solution.py
@@ -6,7 +6,7 @@
 
 def spread_2(block, axis, holder):
     block = jnp.where(lax.axis_index(axis) == holder, block, jnp.zeros_like(block))
-    return lax.psum(block, axis)
+    return jnp.sum(lax.all_gather(block, axis), axis=0)
 
 
 def on_device(lower_sub, upper_sub, block_mask, front_base, pivot_inverse, pivot_order):

time: 362 us -> 230 us (0.64)
  waiting for transfers between devices: 269 us -> 112 us
  blocking collectives: 57.9 us -> 84.6 us
    psum x4 -> x0, waiting for transfers between devices: 228 us -> none  [spread_2(): return lax.psum(block, axis)]
    all_gather x0 -> x2, waiting for transfers between devices: none -> 69.9 us  [spread_2(): return jnp.sum(lax.all_gather(block, axis), axis=0)]
    all_gather x0 -> x2, blocking collectives: none -> 26.8 us  [spread_2(): return jnp.sum(lax.all_gather(block, axis), axis=0)]
  transfers between devices with their start and end apart: 5 -> 3, of which waited for: 5 -> 3; matrix products, arithmetic and copies ran while one was open for 0% -> 0% of each run, Pallas kernels for 0% -> 0%
where the time goes in v1:
time: 230 us; the launch traced here: 228 us
  waiting for transfers between devices  112 us (49%)
  blocking collectives  84.6 us (37%)
  between operations  13.3 us (6%)
  matrix products  10.3 us (4%)
  other arithmetic  5.8 us (3%)
    all_gather x2, waiting for transfers between devices, spread_2(): return jnp.sum(lax.all_gather(block, axis), axis=0)  69.9 us
    all_gather x2, blocking collectives, on_device(): column_rows = lax.all_gather(front, 'gz', axis=0, tiled=True)  57.8 us
    reduce_scatter x1, waiting for transfers between devices, on_device(): lax.psum_scatter(jnp.dot(left_factor, right_factor, preferred_element_typ...  41.6 us
    all_gather x2, blocking collectives, spread_2(): return jnp.sum(lax.all_gather(block, axis), axis=0)  26.8 us
    dot_general x1, matrix products, on_device(): jnp.dot(left_factor, right_factor, preferred_element_type=jnp.float32)  7.75 us
  transfers between devices with their start and end apart: 3, of which 3 were waited for; matrix products, arithmetic and copies ran while one was open for 0% of the time, Pallas kernels for 0%

profile of v1, /device:TPU:8, one launch (start us, length us, event | category | flops | bytes accessed | tf_op | source)
XLA Modules:
  0.0 228.0 jit_solution(11984325215547632033)
XLA Ops:
  6.5 0.0 reduce-scatter.2.cloned.1.call-start
  6.5 0.7 convert_bitcast_fusion
  7.2 0.1 copy.7
  7.3 0.2 broadcast_in_dim.90
  7.5 0.0 copy-start.1
  7.5 0.0 copy-start.2
  7.5 0.0 copy-start
  7.6 7.8 %fusion.3 = f32[512,256]{1,0:T(8,128)} fusion(bf16[1,8192,256]{2,1,0:T(8,128)(2,1)} %param.17, bf16[1,512,8192]{2,1,0:T(8,128)(2,1)} %param.16, f32[64,8,2,128]{3,2,1,0:T(2,128)S(1)} %bitcast.36), kind=kOutput, calls=%fused_computation.5 | convolution fusion | flops 2147614720 | bytes 13631488 | tf_op jit(solution)/shard_map/dot_general | solution.py:25
  15.3 0.0 reduce-scatter.2.cloned.1.call-update
  15.3 0.0 all-gather.7.cloned.1.call-start
  15.4 41.6 %reduce-scatter.2.cloned.1.call-done = f32[64,256]{1,0:T(8,128)} async-done(((f32[512,256]{1,0:T(8,128)}), f32[64,256]{1,0:T(8,128)}) %reduce-scatter.2.cloned.1.call-update) | async-done | bytes 65552 | tf_op jit(solution)/shard_map/reduce_scatter | solution.py:24
  57.0 0.0 copy-done.1
  57.0 0.9 add.73
  57.9 30.0 %all_gather.30 = f32[512,256]{1,0:T(8,128)S(1)} all-gather(f32[64,256]{1,0:T(8,128)S(1)} %add.73), channel_id=1, replica_groups=mesh['gz'=8,'row'=4,'col'=8] {'gz'}, dimensions={0}, use_global_device_ids=true | all-gather | bytes 589824 | tf_op jit(solution)/shard_map/all_gather | solution.py:41
  87.8 0.7 slice_select_fusion.1
  88.6 0.0 all-gather.7.cloned.1.call-update
  88.6 0.0 all-gather.9.cloned.1.call-start
  88.7 0.0 copy-done.2
  88.8 35.8 %all-gather.7.cloned.1.call-done = f32[1024,256]{1,0:T(8,128)} async-done(((f32[256,256]{1,0:T(8,128)}), f32[1024,256]{1,0:T(8,128)}) %all-gather.7.cloned.1.call-update) | async-done | bytes 1048592 | tf_op jit(solution)/shard_map/all_gather | solution.py:9
  124.6 1.3 reduce_sum.36
  125.9 1.0 gather_fusion
  126.9 0.3 convolution_select_fusion.5
  127.2 0.0 copy-done
  127.2 0.2 fusion.11
  127.5 13.4 %all-gather.1 = f32[512,256]{1,0:T(8,128)S(1)} all-gather(f32[64,256]{1,0:T(8,128)S(1)} %fusion.11), channel_id=3, replica_groups=mesh['gz'=8,'row'=4,'col'=8] {'col'}, dimensions={0}, use_global_device_ids=true | all-gather | bytes 589824 | tf_op jit(solution)/shard_map/all_gather | solution.py:9
  140.9 0.4 fusion.10
  141.3 27.9 %all_gather.35 = f32[512,256]{1,0:T(8,128)S(1)} all-gather(f32[64,256]{1,0:T(8,128)S(1)} %fusion.10), channel_id=1, replica_groups=mesh['gz'=8,'row'=4,'col'=8] {'gz'}, dimensions={0}, use_global_device_ids=true | all-gather | bytes 589824 | tf_op jit(solution)/shard_map/all_gather | solution.py:41
  169.1 0.7 slice_select_fusion
  169.9 0.0 all-gather.9.cloned.1.call-update
  170.0 34.1 %all-gather.9.cloned.1.call-done = f32[1024,256]{1,0:T(8,128)} async-done(((f32[256,256]{1,0:T(8,128)}), f32[1024,256]{1,0:T(8,128)}) %all-gather.9.cloned.1.call-update) | async-done | bytes 1048592 | tf_op jit(solution)/shard_map/all_gather | solution.py:9
  204.1 1.3 reduce_sum.38
  205.4 1.0 gather_fusion.1
  206.4 0.4 convolution_select_fusion.2
  206.8 0.2 fusion.9
  207.0 13.4 %all-gather.3 = f32[512,256]{1,0:T(8,128)S(1)} all-gather(f32[64,256]{1,0:T(8,128)S(1)} %fusion.9), channel_id=5, replica_groups=mesh['gz'=8,'row'=4,'col'=8] {'col'}, dimensions={0}, use_global_device_ids=true | all-gather | bytes 589824 | tf_op jit(solution)/shard_map/all_gather | solution.py:9
  220.5 1.0 fusion.8
  (17 shorter events, 0.2 us)
Async XLA Ops:
  6.5 50.5 %reduce-scatter.2.cloned.1.call-start = ((), (), s32[]{:S(2)}) async-start(), calls=%async_computation.1 | async-start | bytes 589824 | tf_op jit(solution)/shard_map/reduce_scatter | solution.py:24
  7.5 49.5 %copy-start.1 = (f32[64,256]{1,0:T(8,128)S(1)}, f32[64,256]{1,0:T(8,128)}, u32[]{:S(2)}) copy-start(f32[64,256]{1,0:T(8,128)} %param.19) | copy-start | bytes 196612
  7.5 81.2 %copy-start.2 = (s32[2,256]{1,0:T(2,128)S(1)}, s32[2,256]{1,0:T(2,128)}, u32[]{:S(2)}) copy-start(s32[2,256]{1,0:T(2,128)} %param.21) | copy-start | bytes 6148
  7.5 119.6 %copy-start = (f32[2,256,256]{2,1,0:T(8,128)S(1)}, f32[2,256,256]{2,1,0:T(8,128)}, u32[]{:S(2)}) copy-start(f32[2,256,256]{2,1,0:T(8,128)} %param.20) | copy-start | bytes 1572868
  15.3 109.2 %all-gather.7.cloned.1.call-start = ((), (), s32[]{:S(2)}) async-start(), calls=%async_computation.2 | async-start | bytes 1310720 | tf_op jit(solution)/shard_map/all_gather | solution.py:9
  88.6 115.5 %all-gather.9.cloned.1.call-start = ((), (), s32[]{:S(2)}) async-start(), calls=%async_computation.3 | async-start | bytes 1310720 | tf_op jit(solution)/shard_map/all_gather | solution.py:9
Sparse Core Ops, SparseCore 0:
  15.5 41.5 reduce-scatter.1
  88.7 35.7 all-gather.6
  170.0 34.0 all-gather.8

commit v2 on v0

--- a/solution.py
+++ b/solution.py
@@ -38,7 +38,9 @@
         targets = start_row + jnp.arange(panel_width, dtype=jnp.int32)
         placer = (targets[:, None] == row_ids[None, :]).astype(jnp.float32)
         owned = (row_ids >= start_row) & (row_ids < after_row)
-        column_rows = lax.all_gather(front, "gz", axis=0, tiled=True)
+        column_rows = jnp.concatenate(
+            lax.all_to_all(jnp.stack([front] * lax.axis_size("gz")), "gz", 0, 0), axis=0
+        )
         pivot_block = spread_2(column_rows[start_row:after_row], "row", 0)
         permuted = jnp.take(pivot_block, pivot_order[panel], axis=0)
         placed = jnp.dot(placer.T, permuted, precision=highest)

time: 362 us -> 330 us (0.912)
  blocking collectives: 57.9 us -> 0 us
  waiting for transfers between devices: 269 us -> 281 us
  starting transfers between devices: 0.17 us -> 12.1 us
    all_gather x2 -> x0, blocking collectives: 57.9 us -> none  [on_device(): column_rows = lax.all_gather(front, 'gz', axis=0, tiled=True)]
    all_to_all x0 -> x2, waiting for transfers between devices: none -> 13.5 us  [on_device(): lax.all_to_all(jnp.stack([front] * lax.axis_size('gz')), 'gz', 0, 0)]
    all_to_all x0 -> x2, starting transfers between devices: none -> 12 us  [on_device(): lax.all_to_all(jnp.stack([front] * lax.axis_size('gz')), 'gz', 0, 0)]
  transfers between devices with their start and end apart: 5 -> 7, of which waited for: 5 -> 7; matrix products, arithmetic and copies ran while one was open for 0% -> 0% of each run, Pallas kernels for 0% -> 0%
where the time goes in v2:
time: 330 us; the launch traced here: 329 us
  waiting for transfers between devices  281 us (85%)
  matrix products  13.4 us (4%)
  between operations  13.3 us (4%)
  starting transfers between devices  12.1 us (4%)
  local copies, waits for them, and re-layouts  5.84 us (2%)
    psum x4, waiting for transfers between devices, spread_2(): return lax.psum(block, axis)  226 us
    reduce_scatter x1, waiting for transfers between devices, on_device(): lax.psum_scatter(jnp.dot(left_factor, right_factor, preferred_element_typ...  41.7 us
    all_to_all x2, waiting for transfers between devices, on_device(): lax.all_to_all(jnp.stack([front] * lax.axis_size('gz')), 'gz', 0, 0)  13.5 us
    all_to_all x2, starting transfers between devices, on_device(): lax.all_to_all(jnp.stack([front] * lax.axis_size('gz')), 'gz', 0, 0)  12 us
    dot_general x1, matrix products, on_device(): jnp.dot(left_factor, right_factor, preferred_element_type=jnp.float32)  7.76 us
  transfers between devices with their start and end apart: 7, of which 7 were waited for; matrix products, arithmetic and copies ran while one was open for 0% of the time, Pallas kernels for 0%

profile of v2, /device:TPU:8, one launch (start us, length us, event | category | flops | bytes accessed | tf_op | source)
XLA Modules:
  0.0 329.1 jit_solution(10025001320919555267)
XLA Ops:
  6.5 0.0 reduce-scatter.2.cloned.1.call-start
  6.5 0.7 convert_bitcast_fusion
  7.2 0.1 copy.7
  7.3 0.2 broadcast_in_dim.90
  7.5 0.0 copy-start.1
  7.5 0.0 copy-start.2
  7.5 0.0 copy-start
  7.6 7.8 %fusion.3 = f32[512,256]{1,0:T(8,128)} fusion(bf16[1,8192,256]{2,1,0:T(8,128)(2,1)} %param.17, bf16[1,512,8192]{2,1,0:T(8,128)(2,1)} %param.16, f32[64,8,2,128]{3,2,1,0:T(2,128)S(1)} %bitcast.32), kind=kOutput, calls=%fused_computation.5 | convolution fusion | flops 2147614720 | bytes 13631488 | tf_op jit(solution)/shard_map/dot_general | solution.py:25
  15.3 0.0 reduce-scatter.2.cloned.1.call-update
  15.3 41.7 %reduce-scatter.2.cloned.1.call-done = f32[64,256]{1,0:T(8,128)} async-done(((f32[512,256]{1,0:T(8,128)}), f32[64,256]{1,0:T(8,128)}) %reduce-scatter.2.cloned.1.call-update) | async-done | bytes 65552 | tf_op jit(solution)/shard_map/reduce_scatter | solution.py:24
  57.0 0.0 copy-done.1
  57.1 0.8 add.81
  57.9 0.8 stack.4
  58.7 6.1 %all-to-all-start = ((f32[8,64,256]{2,1,0:T(8,128)}), f32[8,64,256]{2,1,0:T(8,128)S(1)}, u32[]{:S(2)}, u32[]{:S(2)}) async-start(f32[8,64,256]{2,1,0:T(8,128)} %stack.4), calls=%async_computation.1 | async-start | bytes 1048576 | tf_op jit(solution)/shard_map/all_to_all | solution.py:42
  64.9 0.0 all-reduce.5.cloned.1.call-start
  64.9 0.0 copy-done.2
  65.0 6.8 %all-to-all-done = f32[8,64,256]{2,1,0:T(8,128)S(1)} async-done(((f32[8,64,256]{2,1,0:T(8,128)}), f32[8,64,256]{2,1,0:T(8,128)S(1)}, u32[]{:S(2)}, u32[]{:S(2)}) %all-to-all-start) | async-done | bytes 524320 | tf_op jit(solution)/shard_map/all_to_all | solution.py:42
  71.7 0.7 slice_select_fusion.1
  72.5 0.0 all-reduce.5.cloned.1.call-update
  72.5 0.0 all-reduce.7.cloned.1.call-start
  72.6 50.6 %all-reduce.5.cloned.1.call-done = f32[256,256]{1,0:T(8,128)} async-done(((f32[256,256]{1,0:T(8,128)}), f32[256,256]{1,0:T(8,128)}) %all-reduce.5.cloned.1.call-update) | async-done | bytes 262160 | tf_op jit(solution)/shard_map/psum | solution.py:9
  123.2 1.9 gather_fusion
  125.1 0.3 convolution_select_fusion.5
  125.4 0.0 copy-done
  125.4 0.9 fusion.11
  126.3 0.0 all-reduce.7.cloned.1.call-update
  126.4 62.6 %all-reduce.7.cloned.1.call-done = f32[64,256]{1,0:T(8,128)} async-done(((f32[64,256]{1,0:T(8,128)}), f32[64,256]{1,0:T(8,128)}) %all-reduce.7.cloned.1.call-update) | async-done | bytes 65552 | tf_op jit(solution)/shard_map/psum | solution.py:9
  189.0 1.3 fusion.10
  190.2 0.8 stack.5
  191.1 5.8 %all-to-all-start.1 = ((f32[8,64,256]{2,1,0:T(8,128)}), f32[8,64,256]{2,1,0:T(8,128)S(1)}, u32[]{:S(2)}, u32[]{:S(2)}) async-start(f32[8,64,256]{2,1,0:T(8,128)} %stack.5), calls=%async_computation.2 | async-start | bytes 1048576 | tf_op jit(solution)/shard_map/all_to_all | solution.py:42
  196.9 0.0 all-reduce.9.cloned.1.call-start
  197.0 6.8 %all-to-all-done.1 = f32[8,64,256]{2,1,0:T(8,128)S(1)} async-done(((f32[8,64,256]{2,1,0:T(8,128)}), f32[8,64,256]{2,1,0:T(8,128)S(1)}, u32[]{:S(2)}, u32[]{:S(2)}) %all-to-all-start.1) | async-done | bytes 524320 | tf_op jit(solution)/shard_map/all_to_all | solution.py:42
  203.7 0.7 slice_select_fusion
  204.5 0.0 all-reduce.9.cloned.1.call-update
  204.5 0.0 all-reduce.11.cloned.1.call-start
  204.6 50.3 %all-reduce.9.cloned.1.call-done = f32[256,256]{1,0:T(8,128)} async-done(((f32[256,256]{1,0:T(8,128)}), f32[256,256]{1,0:T(8,128)}) %all-reduce.9.cloned.1.call-update) | async-done | bytes 262160 | tf_op jit(solution)/shard_map/psum | solution.py:9
  254.9 1.9 gather_fusion.1
  256.8 0.4 convolution_select_fusion.2
  257.2 0.9 fusion.9
  258.0 0.0 all-reduce.11.cloned.1.call-update
  258.1 62.6 %all-reduce.11.cloned.1.call-done = f32[64,256]{1,0:T(8,128)} async-done(((f32[64,256]{1,0:T(8,128)}), f32[64,256]{1,0:T(8,128)}) %all-reduce.11.cloned.1.call-update) | async-done | bytes 65552 | tf_op jit(solution)/shard_map/psum | solution.py:9
  320.7 1.9 fusion.8
  (16 shorter events, 0.1 us)
Async XLA Ops:
  6.5 50.5 %reduce-scatter.2.cloned.1.call-start = ((), (), s32[]{:S(2)}) async-start(), calls=%async_computation.3 | async-start | bytes 589824 | tf_op jit(solution)/shard_map/reduce_scatter | solution.py:24
  7.5 49.5 %copy-start.1 = (f32[64,256]{1,0:T(8,128)S(1)}, f32[64,256]{1,0:T(8,128)}, u32[]{:S(2)}) copy-start(f32[64,256]{1,0:T(8,128)} %param.19) | copy-start | bytes 196612
  7.5 57.4 %copy-start.2 = (s32[2,256]{1,0:T(2,128)S(1)}, s32[2,256]{1,0:T(2,128)}, u32[]{:S(2)}) copy-start(s32[2,256]{1,0:T(2,128)} %param.21) | copy-start | bytes 6148
  7.5 117.9 %copy-start = (f32[2,256,256]{2,1,0:T(8,128)S(1)}, f32[2,256,256]{2,1,0:T(8,128)}, u32[]{:S(2)}) copy-start(f32[2,256,256]{2,1,0:T(8,128)} %param.20) | copy-start | bytes 1572868
  58.7 13.0 %all-to-all-start = ((f32[8,64,256]{2,1,0:T(8,128)}), f32[8,64,256]{2,1,0:T(8,128)S(1)}, u32[]{:S(2)}, u32[]{:S(2)}) async-start(f32[8,64,256]{2,1,0:T(8,128)} %stack.4), calls=%async_computation.1 | async-start | bytes 1048576 | tf_op jit(solution)/shard_map/all_to_all | solution.py:42
  64.9 58.3 %all-reduce.5.cloned.1.call-start = ((), (), s32[]{:S(2)}) async-start(), calls=%async_computation.4 | async-start | bytes 524288 | tf_op jit(solution)/shard_map/psum | solution.py:9
  72.5 116.5 %all-reduce.7.cloned.1.call-start = ((), (), s32[]{:S(2)}) async-start(), calls=%async_computation.5 | async-start | bytes 131072 | tf_op jit(solution)/shard_map/psum | solution.py:9
  191.1 12.6 %all-to-all-start.1 = ((f32[8,64,256]{2,1,0:T(8,128)}), f32[8,64,256]{2,1,0:T(8,128)S(1)}, u32[]{:S(2)}, u32[]{:S(2)}) async-start(f32[8,64,256]{2,1,0:T(8,128)} %stack.5), calls=%async_computation.2 | async-start | bytes 1048576 | tf_op jit(solution)/shard_map/all_to_all | solution.py:42
  196.9 58.0 %all-reduce.9.cloned.1.call-start = ((), (), s32[]{:S(2)}) async-start(), calls=%async_computation.6 | async-start | bytes 524288 | tf_op jit(solution)/shard_map/psum | solution.py:9
  204.5 116.2 %all-reduce.11.cloned.1.call-start = ((), (), s32[]{:S(2)}) async-start(), calls=%async_computation.7 | async-start | bytes 131072 | tf_op jit(solution)/shard_map/psum | solution.py:9
Sparse Core Ops, SparseCore 0:
  15.5 41.5 reduce-scatter.1
  72.6 50.5 all-reduce.4
  126.5 62.4 all-reduce.6
  204.6 50.2 all-reduce.8
  258.2 62.4 all-reduce.10
